TPU v7x, 32 devices: a whole 2x2x4 slice. The times are simulated.
32 devices in a mesh: groups: 2 (over x), region: 16 (over z, y, core).
Axes of the slice: x: 2, y: 2, z: 4, core: 2. Of those that a mesh axis runs over, the one named last changes fastest.
Arguments:
- attributes: bfloat16 [16, 16384], P(None, 'region'), may hold values from -6 to 6
- w_in: bfloat16 [16, 512], replicated, may hold values from -1.5 to 1.5
- w_mid: bfloat16 [512, 512], replicated, may hold values from -0.25 to 0.25
- w_out: bfloat16 [2, 512], replicated, may hold values from -0.25 to 0.25
- b_hid: float32 [2, 512], replicated, may hold values from -3 to 3
- b_out: float32 [2], replicated, may hold values from -3 to 3
- downstream: int32 [16384], P('region'), may hold values from -1 to 16383, as said below
- lateral: float32 [4, 32768], P(None, ('groups', 'region')), parts along dimension 1, may hold values from 0.002 to 0.05
- flow_start: float32 [32768], P(('groups', 'region')), parts along dimension 0, may hold values from 0.1 to 2
- cotangent: float32 [4, 32768], P(None, ('groups', 'region')), parts along dimension 1, may hold values from -0.0625 to 0.0625
Outputs:
- flows: float32 [4, 32768], P(None, ('groups', 'region')), parts along dimension 1
- grad_in: float32 [32, 512], P('groups'), parts along dimension 0
- grad_mid: float32 [1024, 512], P('groups'), parts along dimension 0
- grad_out: float32 [4, 512], P('groups'), parts along dimension 0
- grad_bias: float32 [4, 512], P('groups'), parts along dimension 0
There are 2 independent parts, one for each index of `groups`. A program takes and returns all parts, laid end to end along the dimension named above; an argument that names none is the same for every part. Nothing has to cross between parts.
Inputs may be any that keep to these rules, and one draw needn't show every extreme that they name: `downstream`: local reach k of each device (global index minus the device's first) lies in tier k // 64 of 16 tiers. A reach outside a device's last tier points to a reach of the same device 1 to 3 tiers later, or of the last tier; a reach of a device's last tier points to some reach of the next device, and on the last device it is an outlet, -1.
All inputs are finite; a program needn't handle non-finite values.
Results may differ from a plain program's by a relative error of at most 0.0056.
Values sent between devices are 32-bit elements; how exact they have to be, the bound alone decides.
A program may use at most 64 MiB of HBM per device.

v0:
```python
import jax
import jax.numpy as jnp
from jax import lax
from jax.sharding import PartitionSpec as P

LDEP = 4
TIERS = 16
STEPS = 4


RHO_LO = 16.0
RHO_HI = 16000.0
HIGH = lax.Precision.HIGHEST


def passed_along(shard, axis, by):
    count = lax.axis_size(axis)
    pairs = [(i, i + by) for i in range(count) if 0 <= i + by < count]
    return lax.ppermute(shard, axis, pairs)


def prefix(shard, axis, combine, identity, reverse):
    count, place = (lax.axis_size(axis), lax.axis_index(axis))
    everything = jax.tree.map(lambda part: lax.all_gather(part, axis), shard)
    start = jax.tree.map(
        lambda part, zero: jnp.broadcast_to(jnp.asarray(zero, part.dtype), part.shape),
        shard,
        identity,
    )

    def step(k, before):
        at = count - 1 - k if reverse else k
        reached = at > place if reverse else at < place
        new = combine(before, jax.tree.map(lambda part: part[at], everything))
        return jax.tree.map(lambda a, b: jnp.where(reached, a, b), new, before)

    return lax.fori_loop(0, count, step, start)


def coefficients(logits):
    rho = RHO_LO * jnp.exp(jnp.log(RHO_HI / RHO_LO) * jax.nn.sigmoid(logits[0]))
    weight = 0.45 * jax.nn.sigmoid(logits[1])
    denom = rho + 2.0 * (1.0 - weight)
    return (
        (rho - 2.0 * weight) / denom,
        (rho + 2.0 * weight) / denom,
        (2.0 * (1.0 - weight) - rho) / denom,
        2.0 * rho / denom,
    )


def silu_slope(pre):
    sig = jax.nn.sigmoid(pre)
    return sig * (1.0 + pre * (1.0 - sig))


def contract_last(left, right):
    return lax.dot_general(
        left, right, (((1,), (1,)), ((), ())), preferred_element_type=jnp.float32
    )


def contract_first(left, right):
    return lax.dot_general(
        left, right, (((0,), (0,)), ((), ())), preferred_element_type=jnp.float32
    )


def compose(earlier, later):
    return (
        jnp.dot(later[0], earlier[0], precision=HIGH),
        jnp.dot(later[0], earlier[1], precision=HIGH) + later[1],
    )


def push_local(rhs, tables):
    value = rhs
    for hop_ptr, hop_mult in tables:
        value = value + jax.ops.segment_sum(hop_mult * value, hop_ptr, num_segments=rhs.shape[0])
    return value


def pull_local(rhs, tables):
    value = rhs
    for hop_ptr, hop_mult in tables:
        value = value + hop_mult * value[hop_ptr]
    return value


def body(attributes, w_in, w_mid, w_out, b_hid, b_out, downstream, lateral, flow_start, cotangent):
    rows = downstream.shape[0]
    exits = rows // TIERS
    tail = rows - exits
    place = lax.axis_index("region")
    base = place * rows
    local = jnp.arange(rows, dtype=jnp.int32)
    target = downstream - base
    inside = (downstream >= 0) & (target < rows)
    pointer = jnp.where(inside, target, local)
    live = jnp.where(inside, 1.0, 0.0).astype(jnp.float32)
    first_pre = contract_first(w_in, attributes) + b_hid[0][:, None]
    first = jax.nn.silu(first_pre).astype(jnp.bfloat16)
    second_pre = contract_first(w_mid, first) + b_hid[1][:, None]
    second = jax.nn.silu(second_pre).astype(jnp.bfloat16)
    logits = jnp.dot(w_out, second, preferred_element_type=jnp.float32) + b_out[:, None]
    coeffs, coeff_vjp = jax.vjp(coefficients, logits)
    c_new, c_old, c_self, c_lat = coeffs
    tables = []
    hop_ptr = pointer
    hop_mult = jnp.where(inside, c_new[pointer], 0.0)
    for level in range(LDEP):
        tables.append((hop_ptr, hop_mult))
        hop_mult = hop_mult * hop_mult[hop_ptr]
        hop_ptr = hop_ptr[hop_ptr]
    prior = passed_along(downstream[tail:], "region", 1)
    entry = prior - base
    unit = (local[None, :] == (tail + jnp.arange(exits, dtype=jnp.int32))[:, None]).astype(
        jnp.float32
    )
    reach_back = unit
    for hop_ptr, hop_mult in tables:
        reach_back = reach_back + hop_mult[None, :] * reach_back[:, hop_ptr]
    maps = reach_back[:, entry] * c_new[entry][None, :]
    eye = jnp.eye(exits, dtype=jnp.float32)
    empty = jnp.zeros((exits,), jnp.float32)
    start_tail = passed_along(flow_start[tail:], "region", 1)
    states = [flow_start]
    inflows = [
        jax.ops.segment_sum(flow_start * live, pointer, num_segments=rows)
        + jax.ops.segment_sum(start_tail, entry, num_segments=rows)
    ]
    for step in range(STEPS):
        rhs = c_old * inflows[-1] + c_self * states[-1] + c_lat * lateral[step]
        head = jnp.dot(reach_back, rhs, precision=HIGH)
        unused, arriving = prefix((maps, head), "region", compose, (eye, empty), False)
        remote = jax.ops.segment_sum(arriving, entry, num_segments=rows)
        flow = push_local(rhs + c_new * remote, tables)
        states.append(flow)
        inflows.append(jax.ops.segment_sum(flow * live, pointer, num_segments=rows) + remote)
    grad_new = jnp.zeros((rows,), jnp.float32)
    grad_old = jnp.zeros((rows,), jnp.float32)
    grad_self = jnp.zeros((rows,), jnp.float32)
    grad_lat = jnp.zeros((rows,), jnp.float32)
    carry = jnp.zeros((rows,), jnp.float32)
    for step in range(STEPS - 1, -1, -1):
        adjoint = pull_local(cotangent[step] + carry, tables)
        sent = c_new[entry] * adjoint[entry]
        unused, leaving = prefix((maps.T, sent), "region", compose, (eye, empty), True)
        adjoint = adjoint + jnp.dot(leaving, reach_back, precision=HIGH)
        grad_new = grad_new + adjoint * inflows[step + 1]
        grad_old = grad_old + adjoint * inflows[step]
        grad_self = grad_self + adjoint * states[step]
        grad_lat = grad_lat + adjoint * lateral[step]
        if step > 0:
            weighted = c_old * adjoint
            returned = passed_along(weighted[entry], "region", -1)
            carry = c_self * adjoint + weighted[pointer] * live + jnp.pad(returned, (tail, 0))
    (grad_logits,) = coeff_vjp((grad_new, grad_old, grad_self, grad_lat))
    logit_bf = grad_logits.astype(jnp.bfloat16)
    part_out = contract_last(logit_bf, second)
    pre_two = contract_first(w_out, logit_bf) * silu_slope(second_pre)
    pre_two_bf = pre_two.astype(jnp.bfloat16)
    part_mid = contract_last(first, pre_two_bf)
    pre_one = jnp.dot(w_mid, pre_two_bf, preferred_element_type=jnp.float32) * silu_slope(first_pre)
    part_in = contract_last(attributes, pre_one.astype(jnp.bfloat16))
    part_bias = jnp.stack([jnp.sum(pre_one, axis=1), jnp.sum(pre_two, axis=1)])
    grad_in, grad_mid, grad_out, grad_bias = lax.psum(
        (part_in, part_mid, part_out, part_bias), "region"
    )
    flows = jnp.stack(states[1:])
    return (flows, grad_in, grad_mid, grad_out, grad_bias)


def solution(mesh):
    in_specs = (
        P(None, "region"),
        P(),
        P(),
        P(),
        P(),
        P(),
        P("region"),
        P(None, ("groups", "region")),
        P(("groups", "region")),
        P(None, ("groups", "region")),
    )
    out_specs = (
        P(None, ("groups", "region")),
        P("groups", None),
        P("groups", None),
        P("groups", None),
        P("groups", None),
    )
    return jax.shard_map(body, mesh=mesh, in_specs=in_specs, out_specs=out_specs, check_vma=False)
```

profile of v0, /device:TPU:0, one launch (start us, length us, event | category | flops | bytes accessed | tf_op | source)
XLA Modules:
  0.0 639.1 jit_solution(1170251841090344726)
XLA Ops:
  46.2 7.6 %scatter_custom_fusion = f32[1024]{0:T(1024)S(1)} fusion(s32[1024]{0:T(1024)S(1)} %get-tuple-element.1222, f32[1024]{0:T(1024)S(1)} %select_multiply_fusion.7, f32[]{:T(128)} %constant.288.clone.1), kind=kCustom, calls=%fused_computation.271 | custom fusion | flops 1024 | bytes 4100 | tf_op jit(solution)/shard_map/scatter-add | solution.py:129
  98.9 21.5 %all_gather.30 = f32[16,64,64]{2,1,0:T(8,128)S(1)} all-gather(f32[1,64,64]{2,1,0:T(8,128)S(1)} %copy.30), channel_id=1, replica_groups=mesh['groups'=2,'region'=16] {'region'}, dimensions={0}, use_global_device_ids=true | all-gather | bytes 278528 | tf_op jit(solution)/shard_map/all_gather | solution.py:24
  121.9 30.3 %all-reduce.17 = (f32[1024]{0:T(1024)S(1)}, f32[1024]{0:T(1024)S(1)}) all-reduce(f32[1024]{0:T(1024)S(1)} %dynamic-update-slice, f32[1024]{0:T(1024)S(1)} %multiply_dynamic-update-slice_fusion.3), channel_id=2, replica_groups=mesh['groups'=2,'region'=16] {'region'}, use_global_device_ids=true, to_apply=%add.5 | all-reduce | flops 2048 | bytes 16384
  152.3 18.7 %all-gather.4 = f32[1024,64]{1,0:T(8,128)S(1)} all-gather(f32[64,64]{1,0:T(8,128)S(1)} %fusion.76), channel_id=6, replica_groups=mesh['groups'=2,'region'=16] {'region'}, dimensions={0}, use_global_device_ids=true | all-gather | bytes 278528 | tf_op jit(solution)/shard_map/all_gather | solution.py:24
  179.6 4.5 gather_fusion.18
  194.7 7.6 %scatter_fusion = f32[1024]{0:T(1024)S(1)} fusion(f32[1024]{0:T(1024)S(1)} %get-tuple-element.1210, s32[1024]{0:T(1024)S(1)} %get-tuple-element.1222, f32[1024]{0:T(1024)S(1)} %get-tuple-element.1209), kind=kCustom, calls=%fused_computation.42 | custom fusion | flops 1024 | bytes 16384 | tf_op jit(solution)/shard_map/scatter-add | solution.py:79
  202.4 7.6 %scatter_fusion.1 = f32[1024]{0:T(1024)S(1)} fusion(f32[1024]{0:T(1024)S(1)} %scatter_fusion, s32[1024]{0:T(1024)S(1)} %gather_fusion.3, f32[1024]{0:T(1024)S(1)} %get-tuple-element.1258), kind=kCustom, calls=%fused_computation.43 | custom fusion | flops 1024 | bytes 16384 | tf_op jit(solution)/shard_map/scatter-add | solution.py:79
  214.6 7.6 %scatter_fusion.2 = f32[1024]{0:T(1024)S(1)} fusion(f32[1024]{0:T(1024)S(1)} %scatter_fusion.1, s32[1024]{0:T(1024)S(1)} %gather_fusion.6, f32[1024]{0:T(1024)S(1)} %get-tuple-element.1256), kind=kCustom, calls=%fused_computation.44 | custom fusion | flops 1024 | bytes 16384 | tf_op jit(solution)/shard_map/scatter-add | solution.py:79
  226.7 7.6 %scatter_fusion.3 = f32[1024]{0:T(1024)S(1)} fusion(f32[1024]{0:T(1024)S(1)} %scatter_fusion.2, s32[1024]{0:T(1024)S(1)} %gather_fusion.9, f32[1024]{0:T(1024)S(1)} %get-tuple-element.1254), kind=kCustom, calls=%fused_computation.45 | custom fusion | flops 1024 | bytes 16384 | tf_op jit(solution)/shard_map/scatter-add | solution.py:79
  234.4 7.6 %scatter_fusion.4 = f32[1024]{0:T(1024)S(1)} fusion(f32[1024]{0:T(1024)S(1)} %scatter_custom_fusion.2, s32[1024]{0:T(1024)S(1)} %get-tuple-element.1222, f32[1024]{0:T(1024)S(1)} %select_multiply_fusion.6), kind=kCustom, calls=%fused_computation.46 | custom fusion | flops 1024 | bytes 16384 | tf_op jit(solution)/shard_map/scatter-add | solution.py:139
  243.5 32.5 %all-reduce.16 = (f32[1024]{0:T(1024)S(1)}, f32[1024]{0:T(1024)S(1)}) all-reduce(f32[1024]{0:T(1024)S(1)} %dynamic-update-slice.1, f32[1024]{0:T(1024)S(1)} %multiply_dynamic-update-slice_fusion.2), channel_id=3, replica_groups=mesh['groups'=2,'region'=16] {'region'}, use_global_device_ids=true, to_apply=%add.6 | all-reduce | flops 2048 | bytes 16384
  284.6 4.5 gather_fusion.25
  299.4 7.8 %scatter_fusion.5 = f32[1024]{0:T(1024)S(1)} fusion(f32[1024]{0:T(1024)S(1)} %get-tuple-element.1206, s32[1024]{0:T(1024)S(1)} %get-tuple-element.1222, f32[1024]{0:T(1024)S(1)} %get-tuple-element.1205), kind=kCustom, calls=%fused_computation.48 | custom fusion | flops 1024 | bytes 16384 | tf_op jit(solution)/shard_map/scatter-add | solution.py:79
  307.2 7.6 %scatter_fusion.6 = f32[1024]{0:T(1024)S(1)} fusion(f32[1024]{0:T(1024)S(1)} %scatter_fusion.5, s32[1024]{0:T(1024)S(1)} %gather_fusion.3, f32[1024]{0:T(1024)S(1)} %get-tuple-element.1251), kind=kCustom, calls=%fused_computation.49 | custom fusion | flops 1024 | bytes 16384 | tf_op jit(solution)/shard_map/scatter-add | solution.py:79
  319.4 7.6 %scatter_fusion.7 = f32[1024]{0:T(1024)S(1)} fusion(f32[1024]{0:T(1024)S(1)} %scatter_fusion.6, s32[1024]{0:T(1024)S(1)} %gather_fusion.6, f32[1024]{0:T(1024)S(1)} %get-tuple-element.1249), kind=kCustom, calls=%fused_computation.50 | custom fusion | flops 1024 | bytes 16384 | tf_op jit(solution)/shard_map/scatter-add | solution.py:79
  331.5 7.6 %scatter_fusion.8 = f32[1024]{0:T(1024)S(1)} fusion(f32[1024]{0:T(1024)S(1)} %scatter_fusion.7, s32[1024]{0:T(1024)S(1)} %gather_fusion.9, f32[1024]{0:T(1024)S(1)} %get-tuple-element.1247), kind=kCustom, calls=%fused_computation.51 | custom fusion | flops 1024 | bytes 16384 | tf_op jit(solution)/shard_map/scatter-add | solution.py:79
  339.2 7.6 %scatter_fusion.9 = f32[1024]{0:T(1024)S(1)} fusion(f32[1024]{0:T(1024)S(1)} %scatter_custom_fusion.8, s32[1024]{0:T(1024)S(1)} %get-tuple-element.1222, f32[1024]{0:T(1024)S(1)} %select_multiply_fusion.5), kind=kCustom, calls=%fused_computation.52 | custom fusion | flops 1024 | bytes 16384 | tf_op jit(solution)/shard_map/scatter-add | solution.py:139
  348.3 31.1 %all-reduce.15 = (f32[1024]{0:T(1024)S(1)}, f32[1024]{0:T(1024)S(1)}) all-reduce(f32[1024]{0:T(1024)S(1)} %dynamic-update-slice.2, f32[1024]{0:T(1024)S(1)} %multiply_dynamic-update-slice_fusion.1), channel_id=4, replica_groups=mesh['groups'=2,'region'=16] {'region'}, use_global_device_ids=true, to_apply=%add.7 | all-reduce | flops 2048 | bytes 16384
  388.0 4.5 gather_fusion.32
  402.7 7.6 %scatter_fusion.10 = f32[1024]{0:T(1024)S(1)} fusion(f32[1024]{0:T(1024)S(1)} %get-tuple-element.1202, s32[1024]{0:T(1024)S(1)} %get-tuple-element.1222, f32[1024]{0:T(1024)S(1)} %get-tuple-element.1201), kind=kCustom, calls=%fused_computation.54 | custom fusion | flops 1024 | bytes 16384 | tf_op jit(solution)/shard_map/scatter-add | solution.py:79
  410.4 7.8 %scatter_fusion.11 = f32[1024]{0:T(1024)S(1)} fusion(f32[1024]{0:T(1024)S(1)} %scatter_fusion.10, s32[1024]{0:T(1024)S(1)} %gather_fusion.3, f32[1024]{0:T(1024)S(1)} %get-tuple-element.1244), kind=kCustom, calls=%fused_computation.55 | custom fusion | flops 1024 | bytes 16384 | tf_op jit(solution)/shard_map/scatter-add | solution.py:79
  422.8 7.6 %scatter_fusion.12 = f32[1024]{0:T(1024)S(1)} fusion(f32[1024]{0:T(1024)S(1)} %scatter_fusion.11, s32[1024]{0:T(1024)S(1)} %gather_fusion.6, f32[1024]{0:T(1024)S(1)} %get-tuple-element.1242), kind=kCustom, calls=%fused_computation.56 | custom fusion | flops 1024 | bytes 16384 | tf_op jit(solution)/shard_map/scatter-add | solution.py:79
  434.9 7.6 %scatter_fusion.13 = f32[1024]{0:T(1024)S(1)} fusion(f32[1024]{0:T(1024)S(1)} %scatter_fusion.12, s32[1024]{0:T(1024)S(1)} %gather_fusion.9, f32[1024]{0:T(1024)S(1)} %get-tuple-element.1240), kind=kCustom, calls=%fused_computation.57 | custom fusion | flops 1024 | bytes 16384 | tf_op jit(solution)/shard_map/scatter-add | solution.py:79
  442.6 7.6 %scatter_fusion.14 = f32[1024]{0:T(1024)S(1)} fusion(f32[1024]{0:T(1024)S(1)} %scatter_custom_fusion.14, s32[1024]{0:T(1024)S(1)} %get-tuple-element.1222, f32[1024]{0:T(1024)S(1)} %select_multiply_fusion.4), kind=kCustom, calls=%fused_computation.58 | custom fusion | flops 1024 | bytes 16384 | tf_op jit(solution)/shard_map/scatter-add | solution.py:139
  451.7 31.1 %all-reduce.14 = (f32[1024]{0:T(1024)S(1)}, f32[1024]{0:T(1024)S(1)}) all-reduce(f32[1024]{0:T(1024)S(1)} %dynamic-update-slice.3, f32[1024]{0:T(1024)S(1)} %multiply_dynamic-update-slice_fusion), channel_id=5, replica_groups=mesh['groups'=2,'region'=16] {'region'}, use_global_device_ids=true, to_apply=%add.8 | all-reduce | flops 2048 | bytes 16384
  486.8 7.6 %scatter_fusion.15 = f32[1024]{0:T(1024)S(1)} fusion(f32[1024]{0:T(1024)S(1)} %get-tuple-element.1198, s32[1024]{0:T(1024)S(1)} %get-tuple-element.1222, f32[1024]{0:T(1024)S(1)} %get-tuple-element.1197), kind=kCustom, calls=%fused_computation.60 | custom fusion | flops 1024 | bytes 16384 | tf_op jit(solution)/shard_map/scatter-add | solution.py:79
  494.5 7.6 %scatter_fusion.16 = f32[1024]{0:T(1024)S(1)} fusion(f32[1024]{0:T(1024)S(1)} %scatter_fusion.15, s32[1024]{0:T(1024)S(1)} %gather_fusion.3, f32[1024]{0:T(1024)S(1)} %mul.528), kind=kCustom, calls=%fused_computation.61 | custom fusion | flops 1024 | bytes 16384 | tf_op jit(solution)/shard_map/scatter-add | solution.py:79
  502.1 7.6 %scatter_fusion.17 = f32[1024]{0:T(1024)S(1)} fusion(f32[1024]{0:T(1024)S(1)} %scatter_fusion.16, s32[1024]{0:T(1024)S(1)} %gather_fusion.6, f32[1024]{0:T(1024)S(1)} %mul.529), kind=kCustom, calls=%fused_computation.62 | custom fusion | flops 1024 | bytes 16384 | tf_op jit(solution)/shard_map/scatter-add | solution.py:79
  509.8 7.6 %scatter_fusion.18 = f32[1024]{0:T(1024)S(1)} fusion(f32[1024]{0:T(1024)S(1)} %scatter_fusion.17, s32[1024]{0:T(1024)S(1)} %gather_fusion.9, f32[1024]{0:T(1024)S(1)} %mul.530), kind=kCustom, calls=%fused_computation.63 | custom fusion | flops 1024 | bytes 16384 | tf_op jit(solution)/shard_map/scatter-add | solution.py:79
  517.4 7.9 %scatter_fusion.19 = f32[1024]{0:T(1024)S(1)} fusion(f32[1024]{0:T(1024)S(1)} %scatter_custom_fusion.20, s32[1024]{0:T(1024)S(1)} %get-tuple-element.1222, f32[1024]{0:T(1024)S(1)} %select_multiply_fusion), kind=kCustom, calls=%fused_computation.64 | custom fusion | flops 1024 | bytes 16384 | tf_op jit(solution)/shard_map/scatter-add | solution.py:139
  539.8 58.6 %all-reduce.13 = (f32[16,512]{1,0:T(8,128)}, f32[2,512]{1,0:T(2,128)}, f32[2,512]{1,0:T(2,128)}) all-reduce(f32[16,512]{1,0:T(8,128)S(1)} %convolution_bitcast_fusion.8, f32[2,512]{1,0:T(2,128)S(1)} %fusion.124, f32[2,512]{1,0:T(2,128)S(1)} %pad_maximum_fusion.1), channel_id=1, replica_groups=mesh['groups'=2,'region'=16] {'region'}, use_global_device_ids=true, to_apply=%region_42.43 | all-reduce | flops 10240 | bytes 81920 | tf_op jit(solution)/shard_map/psum | solution.py:167
  599.0 30.5 %all-reduce.20.cloned.1.call-done = f32[512,512]{1,0:T(8,128)} async-done(((f32[512,512]{1,0:T(8,128)}), f32[512,512]{1,0:T(8,128)}) %all-reduce.20.cloned.1.call-update) | async-done | bytes 1048592 | tf_op jit(solution)/shard_map/psum | solution.py:167
  (446 shorter events, 217.6 us)
Async XLA Ops:
  7.2 15.3 %copy-start = (bf16[512,512]{1,0:T(8,128)(2,1)S(1)}, bf16[512,512]{1,0:T(8,128)(2,1)}, u32[]{:S(2)}) copy-start(bf16[512,512]{1,0:T(8,128)(2,1)} %param.28) | copy-start | bytes 1572868
  7.2 622.3 %all-reduce.20.cloned.1.call-start = ((), (), s32[]{:S(2)}) async-start(), calls=%async_computation | async-start | bytes 2097152 | tf_op jit(solution)/shard_map/psum | solution.py:167
  8.0 47.1 %collective-permute-start = (s32[64]{0:T(128)S(1)}, s32[64]{0:T(128)S(1)}, u32[]{:S(2)}, u32[]{:S(2)}) collective-permute-start(s32[64]{0:T(128)S(1)} %slice.50), channel_id=1, source_target_pairs={{0,1},{1,2},{2,3},{3,4},{4,5},{5,6},{6,7},{7,8},{8,9},{9,10},{10,1... | collective-permute-start | bytes 776 | tf_op jit(solution)/shard_map/ppermute | solution.py:19
  11.1 44.0 %collective-permute-start.1 = (f32[64]{0:T(128)S(1)}, f32[64]{0:T(128)S(1)}, u32[]{:S(2)}, u32[]{:S(2)}) collective-permute-start(f32[64]{0:T(128)S(1)} %slice.51), channel_id=1, source_target_pairs={{0,1},{1,2},{2,3},{3,4},{4,5},{5,6},{6,7},{7,8},{8,9},{9,10},{10,1... | collective-permute-start | bytes 776 | tf_op jit(solution)/shard_map/ppermute | solution.py:19
  22.5 2.3 copy-start.6
  22.5 2.3 copy-start.3
  22.5 2.3 copy-start.4
  41.6 12.2 %copy-start.5 = (u32[32]{0:T(128)S(1)}, u32[32]{0:T(128)}, u32[]{:S(2)}) copy-start(u32[32]{0:T(128)} %constant.306) | copy-start | bytes 388
  41.6 14.5 %copy-start.1 = (f32[1024]{0:T(1024)S(1)}, f32[1024]{0:T(1024)}, u32[]{:S(2)}) copy-start(f32[1024]{0:T(1024)} %param.34) | copy-start | bytes 12292
  175.3 10.3 %collective-permute-start.2 = (f32[64]{0:T(128)S(1)}, f32[64]{0:T(128)S(1)}, u32[]{:S(2)}, u32[]{:S(2)}) collective-permute-start(f32[64]{0:T(128)S(1)} %gather_fusion.19), channel_id=1, source_target_pairs={{1,0},{2,1},{3,2},{4,3},{5,4},{6,5},{7,6},{8,7},{9,8},{10,9},{11,1... | collective-permute-start | bytes 776 | tf_op jit(solution)/shard_map/ppermute | solution.py:19
  280.4 9.8 %collective-permute-start.3 = (f32[64]{0:T(128)S(1)}, f32[64]{0:T(128)S(1)}, u32[]{:S(2)}, u32[]{:S(2)}) collective-permute-start(f32[64]{0:T(128)S(1)} %gather_fusion.26), channel_id=1, source_target_pairs={{1,0},{2,1},{3,2},{4,3},{5,4},{6,5},{7,6},{8,7},{9,8},{10,9},{11,1... | collective-permute-start | bytes 776 | tf_op jit(solution)/shard_map/ppermute | solution.py:19
  383.8 9.8 %collective-permute-start.4 = (f32[64]{0:T(128)S(1)}, f32[64]{0:T(128)S(1)}, u32[]{:S(2)}, u32[]{:S(2)}) collective-permute-start(f32[64]{0:T(128)S(1)} %gather_fusion.33), channel_id=1, source_target_pairs={{1,0},{2,1},{3,2},{4,3},{5,4},{6,5},{7,6},{8,7},{9,8},{10,9},{11,1... | collective-permute-start | bytes 776 | tf_op jit(solution)/shard_map/ppermute | solution.py:19
  528.9 3.7 copy-start.7
  538.7 0.8 copy-start.2
Sparse Core Ops, SparseCore 0:
  538.8 90.6 all-reduce.19
where the time goes:
time: 648 us; the launch traced here: 639 us
  blocking collectives  224 us (35%)
  other arithmetic  170 us (26%)
  local copies, waits for them, and re-layouts  145 us (22%)
  matrix products  42.1 us (6%)
  waiting for transfers between devices  30.5 us (5%)
  between operations  16.1 us (2%)
  starting transfers between devices  10.8 us (2%)
    unnamed x4, blocking collectives  125 us
    scatter-add x16, other arithmetic, push_local(): jax.ops.segment_sum(hop_mult * value, hop_ptr, num_segments=rhs.shape[0])  122 us
    gather x16, local copies, waits for them, and re-layouts, pull_local(): value = value + hop_mult * value[hop_ptr]  72.4 us
    psum x1, blocking collectives, body(): lax.psum((part_in, part_mid, part_out, part_bias), 'region')  58.6 us
    all_gather x2, blocking collectives, prefix(): everything = jax.tree.map(lambda part: lax.all_gather(part, axis), shard)  40.2 us
    scatter-add x4, other arithmetic, body(): jax.ops.segment_sum(flow * live, pointer, num_segments=rows) + remote  30.7 us
    psum x1, waiting for transfers between devices, body(): lax.psum((part_in, part_mid, part_out, part_bias), 'region')  30.5 us
    dot_general x128, matrix products, compose(): jnp.dot(later[0], earlier[1], precision=HIGH) + later[1]  22.7 us
  transfers between devices with their start and end apart: 6, of which 1 were waited for; matrix products, arithmetic and copies ran while one was open for 10% of the time, Pallas kernels for 0%

commit v1 on v0

v1 whole, which is shorter than its diff:
```python
import functools
import math

import jax
import jax.numpy as jnp
from jax import lax
from jax.experimental import pallas as pl
from jax.experimental.pallas import tpu as pltpu
from jax.sharding import PartitionSpec as P

TIERS = 16
STEPS = 4
RHO_LO = 16.0
RHO_HI = 16000.0
SPAN = math.log(RHO_HI / RHO_LO)
F32 = jnp.float32
BF16 = jnp.bfloat16
CHUNK = 256
MESH = pl.DeviceIdType.MESH


def dot_nn(a, b):
    return lax.dot_general(a, b, (((1,), (0,)), ((), ())), preferred_element_type=F32)


def dot_nt(a, b):
    return lax.dot_general(a, b, (((1,), (1,)), ((), ())), preferred_element_type=F32)


def split(x):
    hi = x.astype(BF16).astype(F32)
    rest = x - hi
    mid = rest.astype(BF16).astype(F32)
    return jnp.concatenate([hi, mid, rest - mid], axis=0).astype(BF16)


def join(y):
    r = y.shape[0] // 3
    return y[:r] + y[r : 2 * r] + y[2 * r : 3 * r]


def onehot(a, b):
    return jnp.where(a == b, 1.0, 0.0).astype(BF16)


def roll_rows(x, by):
    return jnp.concatenate([x[8 - by :], x[: 8 - by]], axis=0)


def poly_tables(coef):
    cols = coef[0].shape[1]
    row = lax.broadcasted_iota(jnp.int32, (8, cols), 0) % 4
    return [jnp.where(row >= k, jnp.broadcast_to(coef[k], (8, cols)), 0.0) for k in range(4)]


def poly_mul(tables, x):
    out = tables[0] * x
    for k in range(1, 4):
        out = out + tables[k] * roll_rows(x, k)
    return out


def sigmoid(v):
    return 1.0 / (1.0 + jnp.exp(-v))


def bit_of(me, b):
    return (me // (1 << b)) % 2


class Stream:
    def __init__(self, me, order, acc, recv, full, ssem, rsem, at):
        self.me, self.order, self.acc, self.recv, self.full = me, order, acc, recv, full
        self.ssem, self.rsem, self.at = ssem, rsem, at
        self.rows = acc.shape[0]
        self.off, self.size, self.slot = 0, self.rows, 0
        self.copy = None

    def partner(self, b):
        return self.me + (1 - 2 * bit_of(self.me, b)) * (1 << b)

    def put(self, src, dst, stage, b):
        self.copy = pltpu.make_async_remote_copy(
            src_ref=src,
            dst_ref=dst,
            send_sem=self.ssem.at[self.at, stage],
            recv_sem=self.rsem.at[self.at, stage],
            device_id={"region": self.partner(b)},
            device_id_type=MESH,
        )
        self.copy.start()

    def scatter_start(self, s):
        b = self.order[s]
        half = self.size // 2
        mine = bit_of(self.me, b)
        give = pl.multiple_of(self.off + (1 - mine) * half, 8)
        self.off = self.off + mine * half
        self.size = half
        self.put(self.acc.at[pl.ds(give, half)], self.recv.at[pl.ds(self.slot, half)], s, b)

    def scatter_end(self, s):
        self.copy.wait()
        own = pl.ds(pl.multiple_of(self.off, 8), self.size)
        total = self.acc[own, :] + self.recv[pl.ds(self.slot, self.size), :]
        self.slot += self.size
        if s == len(self.order) - 1:
            self.full[own, :] = total
        else:
            self.acc[own, :] = total

    def gather_start(self, s):
        b = self.order[len(self.order) - 1 - s]
        own = self.full.at[pl.ds(pl.multiple_of(self.off, 8), self.size)]
        self.put(own, own, len(self.order) + s, b)
        self.off = self.off - bit_of(self.me, b) * self.size
        self.size *= 2

    def gather_end(self, s):
        self.copy.wait()


def kernel(
    n,
    attr_ref, w_in_ref, w_mid_ref, w_out_ref, b_hid_ref, b_out_ref, down_ref, lat_ref, start_ref, cot_ref,
    flows_ref, gin_ref, gmid_ref, gout_ref, gbias_ref,
    pre1, act1, pre2, act2, wmt, grad2, grad1, oh, prior, begun, info, gath, tail_s, tail_r, info_s, info_r,
    acc_a, acc_b, acc_c, rec_a, rec_b, rec_c, full_a, full_b, full_c, red_s, red_r,
):
    rows = down_ref.shape[1]
    hid = w_mid_ref.shape[0]
    exits = rows // TIERS
    tail = rows - exits
    me = lax.axis_index("region")
    base = me * rows

    barrier = pltpu.get_barrier_semaphore()

    def greet(k, c):
        pl.semaphore_signal(barrier, inc=1, device_id={"region": (me + k) % n}, device_id_type=MESH)
        return c

    lax.fori_loop(1, n, greet, 0)
    pl.semaphore_wait(barrier, n - 1)
    onward = (me + 1) % n
    hello = [
        pltpu.make_async_remote_copy(
            src_ref=src, dst_ref=dst, send_sem=tail_s.at[i], recv_sem=tail_r.at[i],
            device_id={"region": onward}, device_id_type=MESH,
        )
        for i, (src, dst) in enumerate(((down_ref, prior), (start_ref, begun)))
    ]
    for copy in hello:
        copy.start()

    columns = jnp.concatenate(
        [b_hid_ref[...], w_out_ref[...].astype(F32), jnp.zeros((4, hid), F32)], axis=0
    ).T
    bias1, bias2 = columns[:, 0:1], columns[:, 1:2]
    w_in_t = w_in_ref[...].T
    wmt[...] = w_mid_ref[...].T

    def forward(c, carry):
        at = pl.ds(pl.multiple_of(c * CHUNK, CHUNK), CHUNK)
        p = dot_nn(w_in_t, attr_ref[:, at]) + bias1
        pre1[:, at] = p
        a = (p * sigmoid(p)).astype(BF16)
        act1[:, at] = a
        q = dot_nn(wmt[...], a) + bias2
        pre2[:, at] = q
        act2[:, at] = (q * sigmoid(q)).astype(BF16)
        return carry

    lax.fori_loop(0, rows // CHUNK, forward, 0)
    logits = dot_nn(w_out_ref[...], act2[...])
    s0 = sigmoid(logits[0:1] + b_out_ref[0])
    s1 = sigmoid(logits[1:2] + b_out_ref[1])
    rho = RHO_LO * jnp.exp(SPAN * s0)
    weight = 0.45 * s1
    denom = rho + 2.0 * (1.0 - weight)
    c_new = (rho - 2.0 * weight) / denom
    c_old = (rho + 2.0 * weight) / denom
    c_self = (2.0 * (1.0 - weight) - rho) / denom
    c_lat = 2.0 * rho / denom

    t1 = c_old + c_self * c_new
    trans = poly_tables([c_new, t1, c_self * t1, c_self * c_self * t1])
    self2 = c_self * c_self
    hold = poly_tables([jnp.ones_like(c_self), c_self, self2, self2 * c_self])

    ptr = down_ref[...] - base
    lane = lax.broadcasted_iota(jnp.int32, (1, rows), 1)
    window = jnp.where(ptr >= tail, ptr - tail + 3 * exits, ptr - exits * (lane // exits + 1))
    slots = lax.broadcasted_iota(jnp.int32, (4 * exits, exits), 0)
    for k in range(TIERS - 1):
        oh[k] = onehot(slots, window[:, k * exits : (k + 1) * exits])

    def tier(x, k):
        return x[:, k * exits : (k + 1) * exits]

    def targets(k):
        return [j if j < TIERS - 1 else None for j in (k + 1, k + 2, k + 3)] + [TIERS - 1]

    cot = cot_ref[...]
    seed = jnp.concatenate([cot[3:4], cot[2:3], cot[1:2], cot[0:1], jnp.zeros((4, rows), F32)], axis=0)
    row8 = lax.broadcasted_iota(jnp.int32, (8, exits), 0)
    pulled = [None] * TIERS
    passed = [None] * TIERS
    exit_of = [None] * TIERS
    stacks = [None] * TIERS
    blank = jnp.zeros((32, exits), BF16)
    for k in range(TIERS - 1, -1, -1):
        if k == TIERS - 1:
            got = jnp.where(row8 == 4, 1.0, 0.0).astype(F32)
            slot = lax.broadcasted_iota(jnp.int32, (8, exits), 1).astype(F32)
        else:
            parts = [blank if j is None else stacks[j] for j in targets(k)]
            res = dot_nn(jnp.concatenate(parts, axis=1), oh[k])
            got = join(res[:24])
            slot = res[24:32]
        pulled[k] = got
        exit_of[k] = slot
        out = poly_mul([tier(x, k) for x in trans], tier(seed, k) + got)
        passed[k] = out
        stacks[k] = jnp.concatenate([split(out), slot.astype(BF16)], axis=0)
    pulled = jnp.concatenate(pulled, axis=1)
    passed = jnp.concatenate(passed, axis=1)
    exit_row = jnp.concatenate(exit_of, axis=1)

    flow0 = start_ref[...]
    wide0 = jnp.broadcast_to(flow0, (8, rows))
    inflow0 = [jnp.zeros((8, exits), F32)] * TIERS
    for k in range(TIERS - 1):
        res = join(dot_nt(split(tier(wide0, k)), oh[k]))
        for p, j in enumerate(targets(k)):
            if j is not None:
                inflow0[j] = inflow0[j] + res[:, p * exits : (p + 1) * exits]
    inflow0 = jnp.concatenate(inflow0, axis=1)

    for copy in hello:
        copy.wait()
    entry = prior[:, tail:] - base
    entry = jnp.where(me > 0, entry, -1)
    enter = onehot(lax.broadcasted_iota(jnp.int32, (rows, exits), 0), entry)
    begun8 = jnp.broadcast_to(begun[:, tail:], (8, exits))
    inflow0 = (inflow0 + join(dot_nt(split(begun8), enter)))[0:1]
    lat = lat_ref[...]
    source = c_lat * lat
    first_source = source[0:1] + c_old * inflow0 + c_self * flow0
    source8 = jnp.concatenate([first_source, source[1:4], jnp.zeros((4, rows), F32)], axis=0)
    local = poly_mul(hold, source8)

    factor = jnp.concatenate([pulled[4:8], jnp.zeros((4, rows), F32)], axis=0)
    factor = poly_tables([factor[k : k + 1] for k in range(4)])
    exit_i = exit_row[0:1].astype(jnp.int32)
    to_exit = onehot(lax.broadcasted_iota(jnp.int32, (exits, rows), 0), exit_i)
    head = join(dot_nt(split(poly_mul(factor, local)), to_exit))
    lead = dot_nn(jnp.concatenate([split(passed), exit_row.astype(BF16)], axis=0), enter)
    packed = jnp.concatenate([join(lead[:24]), head[0:4], lead[24:28]], axis=0)
    packed = jnp.concatenate([packed, jnp.zeros((16, 128 - exits), F32)], axis=1)
    info[...] = packed
    gath[me] = packed

    def tell(k):
        peer = (me + k) % n
        return pltpu.make_async_remote_copy(
            src_ref=info, dst_ref=gath.at[me], send_sem=info_s.at[peer], recv_sem=info_r.at[me],
            device_id={"region": peer}, device_id_type=MESH,
        )

    def tell_start(k, c):
        tell(k).start()
        return c

    def tell_wait(k, c):
        peer = (me + k) % n
        copy = pltpu.make_async_remote_copy(
            src_ref=info, dst_ref=gath.at[peer], send_sem=info_s.at[peer], recv_sem=info_r.at[peer],
            device_id={"region": peer}, device_id_type=MESH,
        )
        copy.wait_send()
        copy.wait_recv()
        return c

    lax.fori_loop(1, n, tell_start, 0)
    lax.fori_loop(1, n, tell_wait, 0)

    side = lax.broadcasted_iota(jnp.int32, (exits, exits), 0)
    zeros4 = jnp.zeros((4, exits), F32)
    zeros8 = jnp.zeros((8, exits), F32)

    def block(i):
        whole = gath[i][:, :exits]
        gain = poly_tables([whole[4 + k : 5 + k] for k in range(4)])
        return whole, gain, onehot(side, whole[12:13].astype(jnp.int32))

    def walk(k, carry):
        arrive, leave, own_arrive, own_leave = carry
        whole, gain, hot = block(k)
        moved = join(dot_nt(split(poly_mul(gain, arrive)), hot))
        arrive = jnp.concatenate([whole[8:12], zeros4], axis=0) + moved
        own_arrive = jnp.where(k + 1 == me, arrive, own_arrive)
        i = n - 1 - k
        whole, gain, hot = block(i)
        fetched = join(dot_nn(split(leave), hot))
        leave = jnp.concatenate([whole[0:4], zeros4], axis=0) + poly_mul(gain, fetched)
        own_leave = jnp.where(i - 1 == me, leave, own_leave)
        return arrive, leave, own_arrive, own_leave

    unused, unused, arrive, leave = lax.fori_loop(0, n - 1, walk, (zeros8, zeros8, zeros8, zeros8))

    remote = join(dot_nn(split(leave), to_exit))
    below = seed + jnp.concatenate([pulled[0:4], jnp.zeros((4, rows), F32)], axis=0) + poly_mul(factor, remote)
    lam = poly_mul(hold, below)

    inside = join(dot_nt(split(arrive), enter))
    inflow = [tier(inside, k) for k in range(TIERS)]
    flow = [None] * TIERS
    for k in range(TIERS):
        out = tier(local, k) + poly_mul([tier(x, k) for x in trans], inflow[k])
        flow[k] = out
        if k < TIERS - 1:
            res = join(dot_nt(split(out), oh[k]))
            for p, j in enumerate(targets(k)):
                if j is not None:
                    inflow[j] = inflow[j] + res[:, p * exits : (p + 1) * exits]
    inflow = jnp.concatenate(inflow, axis=1)
    flow = jnp.concatenate(flow, axis=1)
    flows_ref[...] = flow[0:4]

    dif_new = jnp.zeros((1, rows), F32)
    dif_old = jnp.zeros((1, rows), F32)
    g_lat = jnp.zeros((1, rows), F32)
    for t in range(STEPS):
        adj = lam[3 - t : 4 - t]
        q = flow0 if t == 0 else flow[t - 1 : t]
        i_now = inflow0 if t == 0 else inflow[t - 1 : t]
        dif_new = dif_new + adj * (inflow[t : t + 1] - q)
        dif_old = dif_old + adj * (i_now - q)
        g_lat = g_lat + adj * lat[t : t + 1]
    inv2 = 1.0 / (denom * denom)
    d_rho = (2.0 * dif_new + (2.0 - 4.0 * weight) * dif_old + 4.0 * (1.0 - weight) * g_lat) * inv2
    d_weight = (4.0 * (dif_old - dif_new) + 4.0 * rho * (dif_old + g_lat)) * inv2
    d0 = d_rho * rho * SPAN * s0 * (1.0 - s0)
    d1 = d_weight * 0.45 * s1 * (1.0 - s1)
    logit_bf = jnp.concatenate([d0, d1, jnp.zeros((14, rows), F32)], axis=0).astype(BF16)
    lf = logit_bf.astype(F32)
    info_rows = lf[0:2]
    begun_w = columns
    w0, w1 = begun_w[:, 2:3], begun_w[:, 3:4]

    sum1 = jnp.zeros((hid, 128), F32)
    sum2 = jnp.zeros((hid, 128), F32)
    for c in range(rows // CHUNK):
        at = slice(c * CHUNK, (c + 1) * CHUNK)
        q = pre2[:, at]
        sig = sigmoid(q)
        two = (w0 * info_rows[0:1, at] + w1 * info_rows[1:2, at]) * (sig * (1.0 + q * (1.0 - sig)))
        grad2[:, at] = two.astype(BF16)
        for j in range(0, CHUNK, 128):
            sum2 = sum2 + two[:, j : j + 128]
        p = pre1[:, at]
        sig = sigmoid(p)
        one = dot_nn(w_mid_ref[...], grad2[:, at]) * (sig * (1.0 + p * (1.0 - sig)))
        grad1[:, at] = one.astype(BF16)
        for j in range(0, CHUNK, 128):
            sum1 = sum1 + one[:, j : j + 128]
    half = hid // 2

    def product(c, carry):
        at = pl.ds(pl.multiple_of(c * 128, 128), 128)
        acc_a[at, :] = dot_nt(act1[at, :], grad2[0:half, :])
        acc_b[at, :] = dot_nt(act1[at, :], grad2[half:hid, :])
        return carry

    lax.fori_loop(0, hid // 128, product, 0)
    part_in = dot_nt(attr_ref[...], grad1[...])
    part_out = dot_nt(logit_bf, act2[...])
    bias_rows = [jnp.sum(s.T, axis=0, keepdims=True) for s in (sum1, sum2)]
    last = jnp.concatenate([part_out[0:2]] + bias_rows + [jnp.zeros((4, hid), F32)], axis=0)
    small = [part_in[0:8], part_in[8:16], last]
    tiles = hid // 128
    acc_c[...] = jnp.zeros_like(acc_c)
    for r in range(3):
        for c in range(tiles):
            i = r * tiles + c
            acc_c[8 * i : 8 * i + 8, :] = small[r][:, c * 128 : (c + 1) * 128]

    bits = n.bit_length() - 1
    order = list(range(bits))
    turned = [0] + list(range(2, bits)) + [1]
    streams = [
        Stream(me, order, acc_a, rec_a, full_a, red_s, red_r, 0),
        Stream(me, turned, acc_b, rec_b, full_b, red_s, red_r, 1),
        Stream(me, order, acc_c, rec_c, full_c, red_s, red_r, 2),
    ]
    for s in range(bits):
        for one in streams:
            if s > 0:
                one.scatter_end(s - 1)
            one.scatter_start(s)
    for s in range(bits):
        for one in streams:
            if s > 0:
                one.gather_end(s - 1)
            else:
                one.scatter_end(bits - 1)
            one.gather_start(s)
    for one in streams:
        one.gather_end(bits - 1)
    gmid_ref[:, 0:half] = full_a[...]
    gmid_ref[:, half:hid] = full_b[...]
    for c in range(tiles):
        at = slice(c * 128, (c + 1) * 128)
        gin_ref[0:8, at] = full_c[8 * c : 8 * c + 8, :]
        gin_ref[8:16, at] = full_c[8 * (tiles + c) : 8 * (tiles + c) + 8, :]
        final = full_c[8 * (2 * tiles + c) : 8 * (2 * tiles + c) + 8, :]
        gout_ref[:, at] = final[0:2]
        gbias_ref[:, at] = final[2:4]


def body(n, attributes, w_in, w_mid, w_out, b_hid, b_out, downstream, lateral, flow_start, cotangent):
    rows = downstream.shape[0]
    hid = w_mid.shape[0]
    attrs = w_in.shape[0]
    exits = rows // TIERS
    half = hid // 2
    bits = n.bit_length() - 1
    vmem = pl.BlockSpec(memory_space=pltpu.VMEM)
    smem = pl.BlockSpec(memory_space=pltpu.SMEM)
    wide = [pltpu.VMEM((hid, half), F32)] * 2 + [pltpu.VMEM((8 * n, 128), F32)]
    flops = 2 * rows * hid * (3 * hid + 4 * attrs)
    return pl.pallas_call(
        functools.partial(kernel, n),
        out_shape=(
            jax.ShapeDtypeStruct((STEPS, rows), F32),
            jax.ShapeDtypeStruct((attrs, hid), F32),
            jax.ShapeDtypeStruct((hid, hid), F32),
            jax.ShapeDtypeStruct((2, hid), F32),
            jax.ShapeDtypeStruct((2, hid), F32),
        ),
        in_specs=[vmem] * 5 + [smem] + [vmem] * 4,
        out_specs=(vmem,) * 5,
        scratch_shapes=[
            pltpu.VMEM((hid, rows), F32),
            pltpu.VMEM((hid, rows), BF16),
            pltpu.VMEM((hid, rows), F32),
            pltpu.VMEM((hid, rows), BF16),
            pltpu.VMEM((hid, hid), BF16),
            pltpu.VMEM((hid, rows), BF16),
            pltpu.VMEM((hid, rows), BF16),
            pltpu.VMEM((TIERS - 1, 4 * exits, exits), BF16),
            pltpu.VMEM((1, rows), jnp.int32),
            pltpu.VMEM((1, rows), F32),
            pltpu.VMEM((16, 128), F32),
            pltpu.VMEM((n, 16, 128), F32),
            pltpu.SemaphoreType.DMA((2,)),
            pltpu.SemaphoreType.DMA((2,)),
            pltpu.SemaphoreType.DMA((n,)),
            pltpu.SemaphoreType.DMA((n,)),
        ]
        + wide * 3
        + [pltpu.SemaphoreType.DMA((3, 2 * bits)), pltpu.SemaphoreType.DMA((3, 2 * bits))],
        compiler_params=pltpu.CompilerParams(
            collective_id=0, has_side_effects=True, vmem_limit_bytes=48 * 1024 * 1024
        ),
        cost_estimate=pl.CostEstimate(flops=flops, bytes_accessed=4 << 20, transcendentals=4 * rows * hid),
    )(
        attributes, w_in, w_mid, w_out, b_hid, b_out,
        downstream.reshape(1, rows), lateral, flow_start.reshape(1, rows), cotangent,
    )


def solution(mesh):
    n = mesh.shape["region"]
    in_specs = (
        P(None, "region"),
        P(),
        P(),
        P(),
        P(),
        P(),
        P("region"),
        P(None, ("groups", "region")),
        P(("groups", "region")),
        P(None, ("groups", "region")),
    )
    out_specs = (
        P(None, ("groups", "region")),
        P("groups", None),
        P("groups", None),
        P("groups", None),
        P("groups", None),
    )
    return jax.shard_map(
        functools.partial(body, n), mesh=mesh, in_specs=in_specs, out_specs=out_specs, check_vma=False
    )
```

time: 648 us -> 69 us (0.11); the launches traced: 639 us -> 68.4 us
  blocking collectives: 224 us -> 0 us
  other arithmetic: 170 us -> 0 us
  local copies, waits for them, and re-layouts: 145 us -> 10.1 us
  Pallas kernels: 0 us -> 57.7 us
  matrix products: 42.1 us -> 0 us
  waiting for transfers between devices: 30.5 us -> 0 us
  between operations: 16.1 us -> 0.67 us
  starting transfers between devices: 10.8 us -> 0 us
    scatter-add x26 -> x0, other arithmetic: 166 us -> none  [the longest x16 122 us: push_local(): jax.ops.segment_sum(hop_mult * value, hop_ptr, num_segments=rhs.shape[0])]
    gather x39 -> x0, local copies, waits for them, and re-layouts: 136 us -> none  [the longest x16 72.4 us: pull_local(): value = value + hop_mult * value[hop_ptr]]
    unnamed x4 -> x0, blocking collectives: 125 us -> none
    psum x1 -> x0, blocking collectives: 58.6 us -> none  [body(): lax.psum((part_in, part_mid, part_out, part_bias), 'region')]
    pallas_call x0 -> x1, Pallas kernels: none -> 57.7 us  [body(): pl.pallas_call(functools.partial(kernel, n), out_shape=(jax.ShapeDtypeStr...]
    dot_general x144 -> x0, matrix products: 42.1 us -> none  [the longest x128 22.7 us: compose(): jnp.dot(later[0], earlier[1], precision=HIGH) + later[1]]
    all_gather x2 -> x0, blocking collectives: 40.2 us -> none  [prefix(): everything = jax.tree.map(lambda part: lax.all_gather(part, axis), shard)]
    psum x1 -> x0, waiting for transfers between devices: 30.5 us -> none  [body(): lax.psum((part_in, part_mid, part_out, part_bias), 'region')]
  transfers between devices with their start and end apart: 6 -> 0, of which waited for: 1 -> 0; matrix products, arithmetic and copies ran while one was open for 10% -> 0% of each run, Pallas kernels for 0% -> 0%
where the time goes in v1:
time: 69 us; the launch traced here: 68.4 us
  Pallas kernels  57.7 us (84%)
  local copies, waits for them, and re-layouts  10.1 us (15%)
    pallas_call x1, Pallas kernels, body(): pl.pallas_call(functools.partial(kernel, n), out_shape=(jax.ShapeDtypeStr...  57.7 us
    unnamed x25, local copies, waits for them, and re-layouts  10.1 us

profile of v1, /device:TPU:0, one launch (start us, length us, event | category | flops | bytes accessed | tf_op | source)
XLA Modules:
  0.0 68.4 jit_solution(10270197460882197206)
XLA Ops:
  0.6 0.0 copy-start.8
  0.6 0.0 copy-start.9
  0.7 0.7 copy-done.8
  1.3 0.0 copy-done.9
  1.3 0.0 copy-start
  1.3 1.0 %copy-done = bf16[512,512]{1,0:T(8,128)(2,1)S(1)} copy-done((bf16[512,512]{1,0:T(8,128)(2,1)S(1)}, bf16[512,512]{1,0:T(8,128)(2,1)}, u32[]{:S(2)}) %copy-start) | copy-done | bytes 524312
  2.4 0.0 copy-start.1
  2.4 0.8 %copy-done.1 = bf16[16,1024]{1,0:T(8,128)(2,1)S(1)} copy-done((bf16[16,1024]{1,0:T(8,128)(2,1)S(1)}, bf16[16,1024]{1,0:T(8,128)(2,1)}, u32[]{:S(2)}) %copy-start.1) | copy-done | bytes 32792
  3.1 0.0 copy-start.2
  3.1 0.7 %copy-done.2 = bf16[16,512]{1,0:T(8,128)(2,1)S(1)} copy-done((bf16[16,512]{1,0:T(8,128)(2,1)S(1)}, bf16[16,512]{1,0:T(8,128)(2,1)}, u32[]{:S(2)}) %copy-start.2) | copy-done | bytes 16408
  3.8 0.0 copy-start.3
  3.8 0.7 %copy-done.3 = f32[4,1024]{1,0:T(4,128)S(1)} copy-done((f32[4,1024]{1,0:T(4,128)S(1)}, f32[4,1024]{1,0:T(4,128)}, u32[]{:S(2)}) %copy-start.3) | copy-done | bytes 16408
  4.6 0.0 copy-start.4
  4.6 0.7 %copy-done.4 = f32[4,1024]{1,0:T(4,128)S(1)} copy-done((f32[4,1024]{1,0:T(4,128)S(1)}, f32[4,1024]{1,0:T(4,128)}, u32[]{:S(2)}) %copy-start.4) | copy-done | bytes 16408
  5.3 0.0 copy-start.5
  5.3 0.7 %copy-done.5 = f32[2,512]{1,0:T(2,128)S(1)} copy-done((f32[2,512]{1,0:T(2,128)S(1)}, f32[2,512]{1,0:T(2,128)}, u32[]{:S(2)}) %copy-start.5) | copy-done | bytes 4120
  6.0 0.0 copy-start.6
  6.0 0.7 %copy-done.6 = s32[1024]{0:T(1024)S(1)} copy-done((s32[1024]{0:T(1024)S(1)}, s32[1024]{0:T(1024)}, u32[]{:S(2)}) %copy-start.6) | copy-done | bytes 4120
  6.7 0.0 copy-start.7
  6.7 0.7 %copy-done.7 = f32[1024]{0:T(1024)S(1)} copy-done((f32[1024]{0:T(1024)S(1)}, f32[1024]{0:T(1024)}, u32[]{:S(2)}) %copy-start.7) | copy-done | bytes 4120
  7.3 57.7 %shard_map.137 = (f32[4,1024]{1,0:T(4,128)S(1)}, f32[16,512]{1,0:T(8,128)S(1)}, f32[512,512]{1,0:T(8,128)S(1)}, f32[2,512]{1,0:T(2,128)S(1)}, f32[2,512]{1,0:T(2,128)S(1)}) custom-call(bf16[16,1024]{1,0:T(8,128)(2,1)S(1)} %copy-done.1, bf16[16,512]{1,0:T(8,128)(2,1)S(1)} %copy-done.2, bf16[512,512]{1,0:T(8,128)(2,1)S(1)} %copy-done, ...), custom_call_target="tpu_custom_call" | custom-call | flops 1677721600 | bytes 4194304 | tf_op jit(solution)/shard_map/pallas_call | solution.py:433
  65.1 0.6 copy.20
  65.7 0.6 copy.21
  66.3 1.0 %copy.22 = f32[512,512]{1,0:T(8,128)} copy(f32[512,512]{1,0:T(8,128)S(1)} %get-tuple-element.12) | data formatting | bytes 2097152
  67.3 0.6 copy.23
  67.8 0.6 copy.24
Async XLA Ops:
  0.6 0.7 copy-start.8
  0.6 0.7 copy-start.9
  1.3 1.0 %copy-start = (bf16[512,512]{1,0:T(8,128)(2,1)S(1)}, bf16[512,512]{1,0:T(8,128)(2,1)}, u32[]{:S(2)}) copy-start(bf16[512,512]{1,0:T(8,128)(2,1)} %w_mid_ref.1) | copy-start | bytes 1572868
  2.4 0.8 %copy-start.1 = (bf16[16,1024]{1,0:T(8,128)(2,1)S(1)}, bf16[16,1024]{1,0:T(8,128)(2,1)}, u32[]{:S(2)}) copy-start(bf16[16,1024]{1,0:T(8,128)(2,1)} %attr_ref.1) | copy-start | bytes 98308
  3.1 0.7 %copy-start.2 = (bf16[16,512]{1,0:T(8,128)(2,1)S(1)}, bf16[16,512]{1,0:T(8,128)(2,1)}, u32[]{:S(2)}) copy-start(bf16[16,512]{1,0:T(8,128)(2,1)} %w_in_ref.1) | copy-start | bytes 49156
  3.8 0.7 %copy-start.3 = (f32[4,1024]{1,0:T(4,128)S(1)}, f32[4,1024]{1,0:T(4,128)}, u32[]{:S(2)}) copy-start(f32[4,1024]{1,0:T(4,128)} %lat_ref.1) | copy-start | bytes 49156
  4.6 0.7 %copy-start.4 = (f32[4,1024]{1,0:T(4,128)S(1)}, f32[4,1024]{1,0:T(4,128)}, u32[]{:S(2)}) copy-start(f32[4,1024]{1,0:T(4,128)} %cot_ref.1) | copy-start | bytes 49156
  5.3 0.7 %copy-start.5 = (f32[2,512]{1,0:T(2,128)S(1)}, f32[2,512]{1,0:T(2,128)}, u32[]{:S(2)}) copy-start(f32[2,512]{1,0:T(2,128)} %b_hid_ref.1) | copy-start | bytes 12292
  6.0 0.7 %copy-start.6 = (s32[1024]{0:T(1024)S(1)}, s32[1024]{0:T(1024)}, u32[]{:S(2)}) copy-start(s32[1024]{0:T(1024)} %param.16) | copy-start | bytes 12292
  6.7 0.7 %copy-start.7 = (f32[1024]{0:T(1024)S(1)}, f32[1024]{0:T(1024)}, u32[]{:S(2)}) copy-start(f32[1024]{0:T(1024)} %param.18) | copy-start | bytes 12292

commit v2 on v1

--- a/solution.py
+++ b/solution.py
@@ -16,6 +16,7 @@
 F32 = jnp.float32
 BF16 = jnp.bfloat16
 CHUNK = 256
+CUTS = 4
 MESH = pl.DeviceIdType.MESH
 
 
@@ -64,69 +65,107 @@
     return 1.0 / (1.0 + jnp.exp(-v))
 
 
-def bit_of(me, b):
-    return (me // (1 << b)) % 2
-
-
 class Stream:
     def __init__(self, me, order, acc, recv, full, ssem, rsem, at):
         self.me, self.order, self.acc, self.recv, self.full = me, order, acc, recv, full
-        self.ssem, self.rsem, self.at = ssem, rsem, at
-        self.rows = acc.shape[0]
-        self.off, self.size, self.slot = 0, self.rows, 0
-        self.copy = None
-
-    def partner(self, b):
-        return self.me + (1 - 2 * bit_of(self.me, b)) * (1 << b)
-
-    def put(self, src, dst, stage, b):
-        self.copy = pltpu.make_async_remote_copy(
+        self.ssem, self.rsem, self.at, self.sem = ssem, rsem, at, 0
+        self.off, self.size, self.slot = 0, acc.shape[0], 0
+        self.copies, self.sent = [], []
+
+    def digit(self, group):
+        return (self.me // (1 << group[0])) % (1 << len(group))
+
+    def put(self, src, dst, peer):
+        copy = pltpu.make_async_remote_copy(
             src_ref=src,
             dst_ref=dst,
-            send_sem=self.ssem.at[self.at, stage],
-            recv_sem=self.rsem.at[self.at, stage],
-            device_id={"region": self.partner(b)},
+            send_sem=self.ssem.at[self.at, self.sem],
+            recv_sem=self.rsem.at[self.at, self.sem],
+            device_id={"region": peer},
             device_id_type=MESH,
         )
-        self.copy.start()
+        copy.start()
+        self.sem += 1
+        self.copies.append(copy)
+        self.sent.append(copy)
+
+    def arrived(self):
+        for copy in self.copies:
+            copy.wait_recv()
+        self.copies = []
 
     def scatter_start(self, s):
-        b = self.order[s]
-        half = self.size // 2
-        mine = bit_of(self.me, b)
-        give = pl.multiple_of(self.off + (1 - mine) * half, 8)
-        self.off = self.off + mine * half
-        self.size = half
-        self.put(self.acc.at[pl.ds(give, half)], self.recv.at[pl.ds(self.slot, half)], s, b)
+        group = self.order[s]
+        ways, mine = 1 << len(group), self.digit(group)
+        self.size //= ways
+        for k in range(1, ways):
+            other = (mine + k) % ways
+            give = pl.ds(pl.multiple_of(self.off + other * self.size, 8), self.size)
+            slot = pl.ds(self.slot + (k - 1) * self.size, self.size)
+            self.put(self.acc.at[give], self.recv.at[slot], self.me + (other - mine) * (1 << group[0]))
+        self.off = self.off + mine * self.size
 
     def scatter_end(self, s):
-        self.copy.wait()
+        self.arrived()
         own = pl.ds(pl.multiple_of(self.off, 8), self.size)
-        total = self.acc[own, :] + self.recv[pl.ds(self.slot, self.size), :]
-        self.slot += self.size
+        total = self.acc[own, :]
+        for k in range(1, 1 << len(self.order[s])):
+            total = total + self.recv[pl.ds(self.slot, self.size), :]
+            self.slot += self.size
         if s == len(self.order) - 1:
             self.full[own, :] = total
         else:
             self.acc[own, :] = total
 
     def gather_start(self, s):
-        b = self.order[len(self.order) - 1 - s]
+        group = self.order[len(self.order) - 1 - s]
+        ways, mine = 1 << len(group), self.digit(group)
         own = self.full.at[pl.ds(pl.multiple_of(self.off, 8), self.size)]
-        self.put(own, own, len(self.order) + s, b)
-        self.off = self.off - bit_of(self.me, b) * self.size
-        self.size *= 2
+        for k in range(1, ways):
+            other = (mine + k) % ways
+            self.put(own, own, self.me + (other - mine) * (1 << group[0]))
+        self.off = self.off - mine * self.size
+        self.size *= ways
 
     def gather_end(self, s):
-        self.copy.wait()
+        self.arrived()
+
+    def finish(self):
+        for copy in self.sent:
+            copy.wait_send()
+
+
+def groups_of(n):
+    bits = n.bit_length() - 1
+    rest = [tuple(range(b, min(b + 2, bits))) for b in range(2, bits, 2)]
+    return [(0,), (1,)] + rest, [(0,)] + rest + [(1,)]
 
 
 def kernel(
     n,
-    attr_ref, w_in_ref, w_mid_ref, w_out_ref, b_hid_ref, b_out_ref, down_ref, lat_ref, start_ref, cot_ref,
+    attr_hbm, w_in_hbm, w_mid_hbm, w_out_ref, b_hid_hbm, b_out_ref, down_hbm, lat_hbm, start_hbm, cot_hbm,
     flows_ref, gin_ref, gmid_ref, gout_ref, gbias_ref,
     pre1, act1, pre2, act2, wmt, grad2, grad1, oh, prior, begun, info, gath, tail_s, tail_r, info_s, info_r,
-    acc_a, acc_b, acc_c, rec_a, rec_b, rec_c, full_a, full_b, full_c, red_s, red_r,
+    attr_ref, w_in_ref, w_mid_ref, b_hid_ref, down_ref, lat_ref, start_ref, cot_ref, load_s,
+    acc, rec, full, acc_c, rec_c, full_c, red_s, red_r,
 ):
+    loads = [
+        pltpu.make_async_copy(src, dst, load_s.at[i])
+        for i, (src, dst) in enumerate(
+            (
+                (down_hbm, down_ref),
+                (start_hbm, start_ref),
+                (w_mid_hbm, w_mid_ref),
+                (attr_hbm, attr_ref),
+                (w_in_hbm, w_in_ref),
+                (b_hid_hbm, b_hid_ref),
+                (lat_hbm, lat_ref),
+                (cot_hbm, cot_ref),
+            )
+        )
+    ]
+    for load in loads:
+        load.start()
     rows = down_ref.shape[1]
     hid = w_mid_ref.shape[0]
     exits = rows // TIERS
@@ -150,8 +189,12 @@
         )
         for i, (src, dst) in enumerate(((down_ref, prior), (start_ref, begun)))
     ]
+    for load in loads[:2]:
+        load.wait()
     for copy in hello:
         copy.start()
+    for load in loads[2:]:
+        load.wait()
 
     columns = jnp.concatenate(
         [b_hid_ref[...], w_out_ref[...].astype(F32), jnp.zeros((4, hid), F32)], axis=0
@@ -365,12 +408,13 @@
         grad1[:, at] = one.astype(BF16)
         for j in range(0, CHUNK, 128):
             sum1 = sum1 + one[:, j : j + 128]
-    half = hid // 2
+    wide = hid // CUTS
 
     def product(c, carry):
         at = pl.ds(pl.multiple_of(c * 128, 128), 128)
-        acc_a[at, :] = dot_nt(act1[at, :], grad2[0:half, :])
-        acc_b[at, :] = dot_nt(act1[at, :], grad2[half:hid, :])
+        both = dot_nt(act1[at, :], grad2[...])
+        for i in range(CUTS):
+            acc[i, at, :] = both[:, i * wide : (i + 1) * wide]
         return carry
 
     lax.fori_loop(0, hid // 128, product, 0)
@@ -386,30 +430,30 @@
             i = r * tiles + c
             acc_c[8 * i : 8 * i + 8, :] = small[r][:, c * 128 : (c + 1) * 128]
 
-    bits = n.bit_length() - 1
-    order = list(range(bits))
-    turned = [0] + list(range(2, bits)) + [1]
+    order, turned = groups_of(n)
+    stages = len(order)
     streams = [
-        Stream(me, order, acc_a, rec_a, full_a, red_s, red_r, 0),
-        Stream(me, turned, acc_b, rec_b, full_b, red_s, red_r, 1),
-        Stream(me, order, acc_c, rec_c, full_c, red_s, red_r, 2),
-    ]
-    for s in range(bits):
+        Stream(me, turned if i % 4 == 1 else order, acc.at[i], rec.at[i], full.at[i], red_s, red_r, i)
+        for i in range(CUTS)
+    ] + [Stream(me, order, acc_c, rec_c, full_c, red_s, red_r, CUTS)]
+    for s in range(stages):
         for one in streams:
             if s > 0:
                 one.scatter_end(s - 1)
             one.scatter_start(s)
-    for s in range(bits):
+    for s in range(stages):
         for one in streams:
             if s > 0:
                 one.gather_end(s - 1)
             else:
-                one.scatter_end(bits - 1)
+                one.scatter_end(stages - 1)
             one.gather_start(s)
     for one in streams:
-        one.gather_end(bits - 1)
-    gmid_ref[:, 0:half] = full_a[...]
-    gmid_ref[:, half:hid] = full_b[...]
+        one.gather_end(stages - 1)
+    for one in streams:
+        one.finish()
+    for i in range(CUTS):
+        gmid_ref[:, i * wide : (i + 1) * wide] = full[i]
     for c in range(tiles):
         at = slice(c * 128, (c + 1) * 128)
         gin_ref[0:8, at] = full_c[8 * c : 8 * c + 8, :]
@@ -424,11 +468,11 @@
     hid = w_mid.shape[0]
     attrs = w_in.shape[0]
     exits = rows // TIERS
-    half = hid // 2
-    bits = n.bit_length() - 1
+    sends = 2 * sum((1 << len(group)) - 1 for group in groups_of(n)[0])
     vmem = pl.BlockSpec(memory_space=pltpu.VMEM)
+    hbm = pl.BlockSpec(memory_space=pltpu.HBM)
     smem = pl.BlockSpec(memory_space=pltpu.SMEM)
-    wide = [pltpu.VMEM((hid, half), F32)] * 2 + [pltpu.VMEM((8 * n, 128), F32)]
+    wide = [pltpu.VMEM((CUTS, hid, hid // CUTS), F32)] * 3 + [pltpu.VMEM((8 * n, 128), F32)] * 3
     flops = 2 * rows * hid * (3 * hid + 4 * attrs)
     return pl.pallas_call(
         functools.partial(kernel, n),
@@ -439,7 +483,7 @@
             jax.ShapeDtypeStruct((2, hid), F32),
             jax.ShapeDtypeStruct((2, hid), F32),
         ),
-        in_specs=[vmem] * 5 + [smem] + [vmem] * 4,
+        in_specs=[hbm] * 3 + [vmem, hbm, smem] + [hbm] * 4,
         out_specs=(vmem,) * 5,
         scratch_shapes=[
             pltpu.VMEM((hid, rows), F32),
@@ -458,11 +502,20 @@
             pltpu.SemaphoreType.DMA((2,)),
             pltpu.SemaphoreType.DMA((n,)),
             pltpu.SemaphoreType.DMA((n,)),
+            pltpu.VMEM((attrs, rows), BF16),
+            pltpu.VMEM((attrs, hid), BF16),
+            pltpu.VMEM((hid, hid), BF16),
+            pltpu.VMEM((2, hid), F32),
+            pltpu.VMEM((1, rows), jnp.int32),
+            pltpu.VMEM((STEPS, rows), F32),
+            pltpu.VMEM((1, rows), F32),
+            pltpu.VMEM((STEPS, rows), F32),
+            pltpu.SemaphoreType.DMA((8,)),
         ]
-        + wide * 3
-        + [pltpu.SemaphoreType.DMA((3, 2 * bits)), pltpu.SemaphoreType.DMA((3, 2 * bits))],
+        + wide
+        + [pltpu.SemaphoreType.DMA((CUTS + 1, sends)), pltpu.SemaphoreType.DMA((CUTS + 1, sends))],
         compiler_params=pltpu.CompilerParams(
-            collective_id=0, has_side_effects=True, vmem_limit_bytes=48 * 1024 * 1024
+            collective_id=0, has_side_effects=True, vmem_limit_bytes=60 * 1024 * 1024
         ),
         cost_estimate=pl.CostEstimate(flops=flops, bytes_accessed=4 << 20, transcendentals=4 * rows * hid),
     )(

time: 69 us -> 58.6 us (0.85)
  Pallas kernels: 57.7 us -> 52.2 us
  local copies, waits for them, and re-layouts: 10.1 us -> 5.48 us
    pallas_call x1, Pallas kernels: 57.7 us -> 52.2 us  [body(): pl.pallas_call(functools.partial(kernel, n), out_shape=(jax.ShapeDtypeStr...]
    unnamed x25 -> x11, local copies, waits for them, and re-layouts: 10.1 us -> 5.48 us
where the time goes in v2:
time: 58.6 us; the launch traced here: 58.3 us
  Pallas kernels  52.2 us (89%)
  local copies, waits for them, and re-layouts  5.48 us (9%)
  between operations  0.66 us (1%)
    pallas_call x1, Pallas kernels, body(): pl.pallas_call(functools.partial(kernel, n), out_shape=(jax.ShapeDtypeStr...  52.2 us
    unnamed x11, local copies, waits for them, and re-layouts  5.48 us

profile of v2, /device:TPU:0, one launch (start us, length us, event | category | flops | bytes accessed | tf_op | source)
XLA Modules:
  0.0 58.3 jit_solution(11128974851122244295)
XLA Ops:
  0.6 52.2 %shard_map.137 = (f32[4,1024]{1,0:T(4,128)}, f32[16,512]{1,0:T(8,128)}, f32[512,512]{1,0:T(8,128)}, f32[2,512]{1,0:T(2,128)}, f32[2,512]{1,0:T(2,128)}) custom-call(bf16[16,1024]{1,0:T(8,128)(2,1)} %attr_hbm.1, bf16[16,512]{1,0:T(8,128)(2,1)} %w_in_hbm.1, bf16[512,512]{1,0:T(8,128)(2,1)} %w_mid_hbm.1, bf16[2,512]{1,0:T(2,128)(2,1)} %w_out_ref.1, ...), custom_call_target="tpu_custom_call" | custom-call | flops 1677721600 | bytes 4194304 | tf_op jit(solution)/shard_map/pallas_call | solution.py:477
  52.8 0.0 copy-start
  52.8 1.3 %copy.20 = f32[4,1024]{1,0:T(4,128)} copy(f32[4,1024]{1,0:T(4,128)} %get-tuple-element.10) | data formatting | bytes 32768
  54.2 0.0 copy-done
  54.2 0.6 %copy.21 = f32[16,512]{1,0:T(8,128)} copy(f32[16,512]{1,0:T(8,128)S(1)} %copy-done) | data formatting | bytes 65536
  54.8 0.0 copy-start.2
  54.8 2.3 %copy.22 = f32[512,512]{1,0:T(8,128)} copy(f32[512,512]{1,0:T(8,128)} %get-tuple-element.12) | data formatting | bytes 2097152
  57.0 0.0 copy-done.2
  57.0 0.0 copy-start.1
  57.0 0.6 %copy.23 = f32[2,512]{1,0:T(2,128)} copy(f32[2,512]{1,0:T(2,128)S(1)} %copy-done.2) | data formatting | bytes 8192
  57.6 0.1 copy-done.1
  57.7 0.6 %copy.24 = f32[2,512]{1,0:T(2,128)} copy(f32[2,512]{1,0:T(2,128)S(1)} %copy-done.1) | data formatting | bytes 8192
Async XLA Ops:
  52.8 1.3 %copy-start = (f32[16,512]{1,0:T(8,128)S(1)}, f32[16,512]{1,0:T(8,128)}, u32[]{:S(2)}) copy-start(f32[16,512]{1,0:T(8,128)} %get-tuple-element.11) | copy-start | bytes 98308
  54.8 2.3 %copy-start.2 = (f32[2,512]{1,0:T(2,128)S(1)}, f32[2,512]{1,0:T(2,128)}, u32[]{:S(2)}) copy-start(f32[2,512]{1,0:T(2,128)} %get-tuple-element.13) | copy-start | bytes 12292
  57.0 0.7 %copy-start.1 = (f32[2,512]{1,0:T(2,128)S(1)}, f32[2,512]{1,0:T(2,128)}, u32[]{:S(2)}) copy-start(f32[2,512]{1,0:T(2,128)} %get-tuple-element.14) | copy-start | bytes 12292
